TPU v7x, 512 devices: a whole 4x8x8 slice. The times are simulated.
512 devices in a mesh: bead: 32 (over z, x), space: 16 (over y, core).
Axes of the slice: x: 4, y: 8, z: 8, core: 2. Of those that a mesh axis runs over, the one named last changes fastest.
Arguments:
- positions: float32 [32, 3, 65536], P('bead', None, 'space'), may hold values from -5 to 5
- momenta: float32 [32, 3, 65536], P('bead', None, 'space'), may hold values from -6 to 6
- forces: float32 [32, 3, 65536], P('bead', None, 'space'), may hold values from -6 to 6
- noise: float32 [32, 3, 65536], P('bead', None, 'space'), may hold values from -6 to 6
- species: int32 [65536], P('space'), may hold values from 0 to 3
- block_pairs: int32 [2, 16384], P(None, 'space'), may hold values from 0 to 71, as said below
- pair_count: int32 [16], P('space'), may hold values from 128 to 1024, as said below
- halo_blocks: int32 [2, 64], P(None, 'space'), may hold values from 0 to 63, as said below
Outputs:
- positions_new: float32 [32, 3, 65536], P('bead', None, 'space')
- momenta_new: float32 [32, 3, 65536], P('bead', None, 'space')
- forces_new: float32 [32, 3, 65536], P('bead', None, 'space')
Inputs may be any that keep to these rules, and one draw needn't show every extreme that they name: `block_pairs`: columns 1024 * s to 1024 * (s + 1) - 1 belong to shard s; row 0 is a local block number below 64, row 1 an extended block number of that shard. `pair_count`: some shard uses all 1024 slots. `halo_blocks`: columns 4 * s to 4 * (s + 1) - 1 belong to shard s; the 8 numbers of a shard are distinct local block numbers.
All inputs are finite; a program needn't handle non-finite values.
Results may differ from a plain program's by a relative error of at most 0.0003.
Values sent between devices are 32-bit elements; how exact they have to be, the bound alone decides.
A program may use at most 64 MiB of HBM per device.

v0:
```python
import functools
import math

import jax
import jax.numpy as jnp
import numpy as np
from jax import lax
from jax.experimental import pallas as pl
from jax.experimental.pallas import tpu as pltpu
from jax.sharding import PartitionSpec as P

BLOCK = 64
LANES = 128
HALO = 4
UNROLL = 4
STEP = 0.5
GAMMA = 0.5
mass_values = (1.0, 0.3, 2.5, 0.75)
strength_values = (1.0, 0.5, 1.5, 0.8)
reach_values = (1.0, 0.6, 1.4, 0.9)
MESH = pl.DeviceIdType.MESH
highest = lax.Precision.HIGHEST


def lookup(values, species):
    out = jnp.full(species.shape, values[3], jnp.float32)
    for k in range(3):
        out = jnp.where(species == k, values[k], out)
    return out


def modes_matrix(n):
    j = np.arange(n)[:, None]
    k = np.arange(n)[None, :]
    phase = 2 * np.pi * (j * k % n) / n
    m = np.where(k < n // 2, np.cos(phase), np.sin(phase)) * math.sqrt(2.0 / n)
    m = np.where(k == 0, math.sqrt(1.0 / n), m)
    m = np.where(k == n // 2, np.where(j % 2 == 0, 1, -1) * math.sqrt(1.0 / n), m)
    return m.astype(np.float32)


def mode_factors(n):
    k = np.arange(n)
    omega = 2 * np.sin(np.pi * k / n)
    gamma = np.where(k == 0, GAMMA, 2 * omega)
    c1 = np.exp(-gamma * STEP)
    c2 = np.sqrt(1 - c1 * c1)
    safe = np.where(k == 0, 1.0, omega)
    drift = np.where(k == 0, STEP, np.sin(omega * STEP) / safe)
    pull = omega * np.sin(omega * STEP)
    turn = np.cos(omega * STEP)
    out = np.zeros((n, LANES), np.float32)
    for c, v in enumerate((c1, c2, turn, drift, pull)):
        out[:, c] = v
    return out


def exchange_kernel(pos_ref, mom_ref, frc_ref, noise_ref, sp_ref, halo_ref, cos_ref, cost_ref, fac_ref,
                    pm_ref, lo_ref, up_ref, slo_ref, sup_ref, hlo_ref, hup_ref,
                    out_buf, in_buf, back_buf, send1, recv1, send2, recv2, nsend, nrecv):
    beads = in_buf.shape[0]
    me = lax.axis_index("bead")
    shard = lax.axis_index("space")
    shards = lax.axis_size("space")
    has_lower = shard > 0
    has_upper = shard < shards - 1

    barrier = pltpu.get_barrier_semaphore()

    def greet(d, _):
        pl.semaphore_signal(barrier, inc=1, device_id={"bead": lax.rem(me + d, beads)}, device_id_type=MESH)
        return 0

    lax.fori_loop(1, beads, greet, 0)

    @pl.when(has_lower)
    def _():
        pl.semaphore_signal(barrier, inc=1, device_id={"space": shard - 1}, device_id_type=MESH)

    @pl.when(has_upper)
    def _():
        pl.semaphore_signal(barrier, inc=1, device_id={"space": shard + 1}, device_id_type=MESH)

    for j in range(beads):
        s = slice(LANES * j, LANES * (j + 1))
        out_buf[j, 0:3] = pos_ref[0, :, s]
        out_buf[j, 3:6] = mom_ref[0, :, s] + (0.5 * STEP) * frc_ref[0, :, s]
        out_buf[j, 6:9] = noise_ref[0, :, s]

    pl.semaphore_wait(barrier, beads - 1 + has_lower.astype(jnp.int32) + has_upper.astype(jnp.int32))

    def first(d):
        j = lax.rem(me + d, beads)
        return pltpu.make_async_remote_copy(
            src_ref=out_buf.at[j, 0:9], dst_ref=in_buf.at[me, 0:9], send_sem=send1.at[j], recv_sem=recv1.at[me],
            device_id={"bead": j}, device_id_type=MESH)

    def second(d):
        j = lax.rem(me + d, beads)
        return pltpu.make_async_remote_copy(
            src_ref=back_buf.at[j, 0:6], dst_ref=pm_ref.at[me, 0:6], send_sem=send2.at[j], recv_sem=recv2.at[me],
            device_id={"bead": j}, device_id_type=MESH)

    def arrived(buf, rows, sem, d):
        j = lax.rem(me + d, beads)
        pltpu.make_async_copy(buf.at[j, 0:rows], buf.at[j, 0:rows], sem.at[j]).wait()

    def each(body):
        def run(d, _):
            body(d)
            return 0
        lax.fori_loop(1, beads, run, 0)

    each(lambda d: first(d).start())
    in_buf[me] = out_buf[me]

    def towards(up):
        to = shard + 1 if up else shard - 1
        k = 3 * int(up)
        ids = {"space": to}

        def copy(src, dst, n):
            return pltpu.make_async_remote_copy(
                src_ref=src, dst_ref=dst, send_sem=nsend.at[k + n], recv_sem=nrecv.at[k + n], device_id=ids,
                device_id_type=MESH)

        def kinds():
            return copy(sp_ref, slo_ref if up else sup_ref, 0)

        def lists():
            return copy(halo_ref, hlo_ref if up else hup_ref, 1)

        def places():
            return copy(pm_ref.at[:, 0:3], lo_ref.at[:, 0:3] if up else up_ref.at[:, 0:3], 2)

        return kinds, lists, places

    for up, there in ((True, has_upper), (False, has_lower)):
        @pl.when(there)
        def _(up=up):
            for c in towards(up)[0:2]:
                c().start()

    each(lambda d: arrived(in_buf, 9, recv1, d))

    def rows(r):
        return in_buf[:, r, :]

    x = jnp.concatenate([rows(r) for r in range(6)], axis=1)
    xi = jnp.concatenate([rows(r) for r in range(6, 9)], axis=1)
    modes = jnp.dot(cost_ref[...], x, precision=highest, preferred_element_type=jnp.float32)
    q, p = modes[:, 0:3 * LANES], modes[:, 3 * LANES:]
    mass = lookup(mass_values, sp_ref[pl.ds(me, 1), :])
    mass3 = jnp.concatenate([mass] * 3, axis=1)
    c1, c2, turn, drift, pull = (fac_ref[:, c:c + 1] for c in range(5))
    mixed = c1 * p + c2 * (jnp.sqrt(mass3) * xi)
    q_next = turn * q + drift * (mixed / mass3)
    p_next = turn * mixed - pull * (mass3 * q)
    beads_out = jnp.dot(cos_ref[...], jnp.concatenate([q_next, p_next], axis=1), precision=highest,
                        preferred_element_type=jnp.float32)
    for r in range(6):
        back_buf[:, r, :] = beads_out[:, LANES * r:LANES * (r + 1)]

    each(lambda d: second(d).start())
    pm_ref[me, 0:6] = back_buf[me, 0:6]
    each(lambda d: arrived(pm_ref, 6, recv2, d))

    for up, there in ((True, has_upper), (False, has_lower)):
        @pl.when(there)
        def _(up=up):
            towards(up)[2]().start()

    each(lambda d: first(d).wait_send())
    each(lambda d: second(d).wait_send())

    for up, there in ((True, has_upper), (False, has_lower)):
        @pl.when(there)
        def _(up=up):
            for c in towards(up):
                c().wait_send()

    for up, there in ((True, has_lower), (False, has_upper)):
        @pl.when(there)
        def _(up=up):
            for c in towards(up):
                c().wait_recv()


def exchange(pos, mom, frc, noise, species, halo):
    beads = lax.axis_size("bead")
    chunks = species.shape[0]
    vmem = pl.BlockSpec(memory_space=pltpu.VMEM)
    f32, i32 = jnp.float32, jnp.int32
    block = jax.ShapeDtypeStruct((chunks, 8, LANES), f32)
    kind = jax.ShapeDtypeStruct(species.shape, i32)
    ids = jax.ShapeDtypeStruct(halo.shape, i32)
    dma = pltpu.SemaphoreType.DMA
    matrix = modes_matrix(beads)
    return pl.pallas_call(
        exchange_kernel,
        out_shape=(block, block, block, kind, kind, ids, ids),
        in_specs=[vmem] * 9,
        out_specs=(vmem,) * 7,
        scratch_shapes=[
            pltpu.VMEM((beads, 16, LANES), f32),
            pltpu.VMEM((beads, 16, LANES), f32),
            pltpu.VMEM((beads, 8, LANES), f32),
            dma((beads,)), dma((beads,)), dma((beads,)), dma((beads,)), dma((6,)), dma((6,)),
        ],
        compiler_params=pltpu.CompilerParams(collective_id=0, has_side_effects=True),
        name="exchange",
    )(pos, mom, frc, noise, species, halo, jnp.asarray(matrix), jnp.asarray(matrix.T), jnp.asarray(mode_factors(beads)))


def force_kernel(pairs_ref, count_ref, hlo_ref, hup_ref, pm_ref, lo_ref, up_ref, sp_ref, slo_ref, sup_ref,
                 pos_ref, mom_ref, frc_ref, tab_j, tab_i, acc, tmp):
    chunks = pm_ref.shape[0]
    blocks = 2 * chunks
    lane = lax.broadcasted_iota(jnp.int32, (32, 128), 1)
    left = lane < 64
    left1 = left[0:8]

    def spread(cols, e):
        for c in range(5):
            b = jnp.broadcast_to(cols[:, c:c + 1], (64, 128))
            tab_j[e, c] = jnp.where(left, b[0:32], b[32:64])

    def packed(rows, species, t):
        xyz = rows[0:3]
        r = lookup(reach_values, species)
        a = lookup(strength_values, species)
        return jnp.concatenate([xyz, r, a, jnp.zeros((3, 128), jnp.float32)], axis=0)

    def own(t, _):
        rows = pm_ref[t]
        m8 = packed(rows, sp_ref[pl.ds(t, 1), :], t)
        cols = m8.T
        spread(cols[0:64], HALO + 2 * t)
        spread(cols[64:128], HALO + 2 * t + 1)
        turned = pltpu.roll(m8, 64, 1)
        for h in range(2):
            both = jnp.where(left1, m8, turned) if h == 0 else jnp.where(left1, turned, m8)
            for c in range(4):
                tab_i[2 * t + h, c] = jnp.broadcast_to(both[c:c + 1], (8, 128))
        for h in range(2):
            for c in range(3):
                acc[2 * t + h, c] = jnp.zeros((8, 128), jnp.float32)
        return 0
    lax.fori_loop(0, chunks, own, 0)

    for side in range(2):
        ids = hlo_ref if side == 0 else hup_ref
        x_ref = lo_ref if side == 0 else up_ref
        s_ref = slo_ref if side == 0 else sup_ref
        there = lax.axis_index("space") > 0 if side == 0 else lax.axis_index("space") < lax.axis_size("space") - 1
        for h in range(HALO):
            b = jnp.where(there, ids[1 - side, h], 0)
            t = b // 2
            m8 = packed(x_ref[t], s_ref[pl.ds(t, 1), :], t)
            m8 = jnp.where(there, m8, 0.0)
            tmp[...] = m8.T
            cols = tmp[pl.ds(pl.multiple_of((b % 2) * 64, 64), 64), :]
            spread(cols, h if side == 0 else HALO + blocks + h)
    tab_j[2 * HALO + blocks] = jnp.zeros(tab_j.shape[1:], jnp.float32)

    live = count_ref[0]

    def pair(p):
        i = pairs_ref[0, p]
        j = jnp.where(p < live, pairs_ref[1, p], 2 * HALO + blocks)
        xi, yi, zi, ri = (tab_i[i, c] for c in range(4))
        f = [None] * 3
        for g in range(4):
            s = pl.ds(8 * g, 8)
            dx = xi - tab_j[j, 0, s]
            dy = yi - tab_j[j, 1, s]
            dz = zi - tab_j[j, 2, s]
            d = dx * dx + dy * dy + dz * dz
            inv = 1.0 / (ri + tab_j[j, 3, s])
            w = jnp.exp(-d * inv) * (inv * tab_j[j, 4, s])
            for k, v in enumerate((dx, dy, dz)):
                f[k] = w * v if g == 0 else f[k] + w * v
        for k in range(3):
            acc[i, k] = acc[i, k] + f[k]

    def group(g, _):
        for u in range(UNROLL):
            pair(g * UNROLL + u)
        return 0
    lax.fori_loop(0, (live + UNROLL - 1) // UNROLL, group, 0)

    def finish(t, _):
        rows = pm_ref[t]
        scale = 0.02 * lookup(strength_values, sp_ref[pl.ds(t, 1), :])
        out = []
        for k in range(3):
            v = [jnp.sum(acc[2 * t + h, k], axis=0, keepdims=True) for h in range(2)]
            v = [x + pltpu.roll(x, 64, 1) for x in v]
            out.append(jnp.where(left[0:1], v[0], v[1]) * scale)
        f = jnp.concatenate(out, axis=0)
        s = pl.ds(pl.multiple_of(t * 128, 128), 128)
        pos_ref[0, :, s] = rows[0:3]
        frc_ref[0, :, s] = f
        mom_ref[0, :, s] = rows[3:6] + 0.25 * f
        return 0
    lax.fori_loop(0, chunks, finish, 0)


def force_call(pairs, count, hlo, hup, pm, lo, up, sp, slo, sup):
    chunks = pm.shape[0]
    smem = pl.BlockSpec(memory_space=pltpu.SMEM)
    vmem = pl.BlockSpec(memory_space=pltpu.VMEM)
    o = jax.ShapeDtypeStruct((1, 3, chunks * 128), jnp.float32)
    return pl.pallas_call(
        force_kernel,
        out_shape=(o, o, o),
        in_specs=[smem] * 4 + [vmem] * 6,
        out_specs=(vmem,) * 3,
        scratch_shapes=[
            pltpu.VMEM((2 * chunks + 2 * HALO + 1, 5, 32, 128), jnp.float32),
            pltpu.VMEM((2 * chunks, 4, 8, 128), jnp.float32),
            pltpu.VMEM((2 * chunks, 3, 8, 128), jnp.float32),
            pltpu.VMEM((128, 8), jnp.float32),
        ],
        compiler_params=pltpu.CompilerParams(vmem_limit_bytes=40 * 2**20),
        name="pair_forces",
    )(pairs, count, hlo, hup, pm, lo, up, sp, slo, sup)


def shards(positions, momenta, forces, noise, species, block_pairs, pair_count, halo_blocks):
    kinds = species.reshape(-1, LANES)
    pm, lo, up, slo, sup, hlo, hup = exchange(positions, momenta, forces, noise, kinds, halo_blocks)
    return force_call(block_pairs, pair_count, hlo, hup, pm, lo, up, kinds, slo, sup)


def solution(mesh):
    big = P("bead", None, "space")
    in_specs = (big, big, big, big, P("space"), P(None, "space"), P("space"), P(None, "space"))
    return jax.shard_map(shards, mesh=mesh, in_specs=in_specs, out_specs=(big, big, big), check_vma=False)
```

profile of v0, /device:TPU:24, one launch (start us, length us, event | category | flops | bytes accessed | tf_op | source)
XLA Modules:
  0.0 72.4 jit_solution(10930225973752195748)
XLA Ops:
  0.6 0.0 copy-start.9
  0.6 1.5 %copy.14.pos_ref = f32[1,3,4096]{2,1,0:T(4,128)} copy(f32[1,3,4096]{2,0,1:T(1,128)} %param.11) | data formatting | bytes 98304 | tf_op args[0]
  2.1 0.0 copy-done.9
  2.1 0.0 copy-start.10
  2.1 0.7 copy.15.mom_ref
  2.8 0.1 copy-done.10
  2.9 0.0 copy-start.11
  2.9 0.6 copy.16.frc_ref
  3.6 0.1 copy-done.11
  3.7 0.7 copy.17.noise_ref
  4.4 0.0 copy-start.3
  4.4 31.6 %exchange.1 = (f32[32,8,128]{2,1,0:T(8,128)}, f32[32,8,128]{2,1,0:T(8,128)}, f32[32,8,128]{2,1,0:T(8,128)}, s32[32,128]{1,0:T(8,128)}, s32[32,128]{1,0:T(8,128)}, /*index=5*/s32[2,4]{1,0:T(2,128)}, s32[2,4]{1,0:T(2,128)}) custom-call(f32[1,3,4096]{2,1,0:T(4,128)} %copy.14.pos_ref, f32[1,3,4096]{2,1,0:T(4,128)} %copy.15.mom_ref, f32[1,3,4096]{2,1,0:T(4,128)} %copy.16.frc_ref, ...), custom_call_target="tpu_custom_call" | custom-call | tf_op jit(solution)/shard_map/exchange/pallas_call | solution.py:199
  35.9 0.0 copy-start.6
  35.9 0.0 copy-start.8
  36.0 0.0 copy-start.7
  36.6 0.0 copy-done.3
  36.6 0.0 copy-done.6
  36.6 0.0 copy-done.8
  36.6 0.0 copy-done.7
  36.7 0.0 copy-start
  36.7 0.9 %copy-done = f32[32,8,128]{2,1,0:T(8,128)S(1)} copy-done((f32[32,8,128]{2,1,0:T(8,128)S(1)}, f32[32,8,128]{2,1,0:T(8,128)}, u32[]{:S(2)}) %copy-start) | copy-done | bytes 131096
  37.6 0.0 copy-start.1
  37.6 0.9 %copy-done.1 = f32[32,8,128]{2,1,0:T(8,128)S(1)} copy-done((f32[32,8,128]{2,1,0:T(8,128)S(1)}, f32[32,8,128]{2,1,0:T(8,128)}, u32[]{:S(2)}) %copy-start.1) | copy-done | bytes 131096
  38.5 0.0 copy-start.2
  38.5 0.9 %copy-done.2 = f32[32,8,128]{2,1,0:T(8,128)S(1)} copy-done((f32[32,8,128]{2,1,0:T(8,128)S(1)}, f32[32,8,128]{2,1,0:T(8,128)}, u32[]{:S(2)}) %copy-start.2) | copy-done | bytes 131096
  39.4 0.0 copy-start.4
  39.4 0.7 copy-done.4
  40.1 0.0 copy-start.5
  40.1 0.7 copy-done.5
  40.8 29.6 %pair_forces.1 = (f32[1,3,4096]{2,1,0:T(4,128)S(1)}, f32[1,3,4096]{2,1,0:T(4,128)S(1)}, f32[1,3,4096]{2,1,0:T(4,128)S(1)}) custom-call(s32[2,1024]{1,0:T(2,128)S(1)} %copy-done.6, s32[1]{0:T(128)S(6)} %copy.21.count_ref, s32[2,4]{1,0:T(2,128)S(1)} %copy-done.7, s32[2,4]{1,0:T(2,128)S(1)} %copy-done.8, f32[32,8,128]{2,1,0:T(8,128)S(1)} %copy-done, ...), custom_call_target="tpu_custom_call" | custom-call | tf_op jit(solution)/shard_map/pair_forces/pallas_call | solution.py:314
  70.4 0.7 copy.18
  71.0 0.7 copy.19
  71.7 0.7 copy.20
Async XLA Ops:
  0.6 1.5 %copy-start.9 = (f32[1,3,4096]{2,0,1:T(1,128)S(1)}, f32[1,3,4096]{2,0,1:T(1,128)}, u32[]{:S(2)}) copy-start(f32[1,3,4096]{2,0,1:T(1,128)} %param.12) | copy-start | bytes 147460
  2.1 0.8 %copy-start.10 = (f32[1,3,4096]{2,0,1:T(1,128)S(1)}, f32[1,3,4096]{2,0,1:T(1,128)}, u32[]{:S(2)}) copy-start(f32[1,3,4096]{2,0,1:T(1,128)} %param.13) | copy-start | bytes 147460
  2.9 0.8 %copy-start.11 = (f32[1,3,4096]{2,0,1:T(1,128)S(1)}, f32[1,3,4096]{2,0,1:T(1,128)}, u32[]{:S(2)}) copy-start(f32[1,3,4096]{2,0,1:T(1,128)} %param.14) | copy-start | bytes 147460
  4.4 32.3 %copy-start.3 = (s32[4096]{0:T(1024)S(1)}, s32[4096]{0:T(1024)}, u32[]{:S(2)}) copy-start(s32[4096]{0:T(1024)} %param.15) | copy-start | bytes 49156
  35.9 0.7 copy-start.6
  35.9 0.7 copy-start.8
  36.0 0.7 copy-start.7
  36.7 0.9 %copy-start = (f32[32,8,128]{2,1,0:T(8,128)S(1)}, f32[32,8,128]{2,1,0:T(8,128)}, u32[]{:S(2)}) copy-start(f32[32,8,128]{2,1,0:T(8,128)} %get-tuple-element.12.pm_ref) | copy-start | bytes 393220
  37.6 0.9 %copy-start.1 = (f32[32,8,128]{2,1,0:T(8,128)S(1)}, f32[32,8,128]{2,1,0:T(8,128)}, u32[]{:S(2)}) copy-start(f32[32,8,128]{2,1,0:T(8,128)} %get-tuple-element.13.lo_ref) | copy-start | bytes 393220
  38.5 0.9 %copy-start.2 = (f32[32,8,128]{2,1,0:T(8,128)S(1)}, f32[32,8,128]{2,1,0:T(8,128)}, u32[]{:S(2)}) copy-start(f32[32,8,128]{2,1,0:T(8,128)} %get-tuple-element.14.up_ref) | copy-start | bytes 393220
  39.4 0.7 copy-start.4
  40.1 0.7 copy-start.5
where the time goes:
time: 73 us; the launch traced here: 72.4 us
  Pallas kernels  61.1 us (84%)
  local copies, waits for them, and re-layouts  9.89 us (14%)
  between operations  1.37 us (2%)
    pallas_call x1, Pallas kernels, exchange(): pl.pallas_call(exchange_kernel, out_shape=(block, block, block, kind, kin...  31.6 us
    pallas_call x1, Pallas kernels, force_call(): pl.pallas_call(force_kernel, out_shape=(o, o, o), in_specs=[smem] * 4 + [...  29.6 us
    unnamed x28, local copies, waits for them, and re-layouts  7.88 us
    pallas_call x3, local copies, waits for them, and re-layouts, force_call(): pl.pallas_call(force_kernel, out_shape=(o, o, o), in_specs=[smem] * 4 + [...  2.01 us

commit v1 on v0

v1 whole, which is shorter than its diff:
```python
import functools
import math

import jax
import jax.numpy as jnp
import numpy as np
from jax import lax
from jax.experimental import pallas as pl
from jax.experimental.pallas import tpu as pltpu
from jax.sharding import PartitionSpec as P

BLOCK = 64
LANES = 128
HALO = 4
UNROLL = 4
STEP = 0.5
GAMMA = 0.5
mass_values = (1.0, 0.3, 2.5, 0.75)
strength_values = (1.0, 0.5, 1.5, 0.8)
reach_values = (1.0, 0.6, 1.4, 0.9)
MESH = pl.DeviceIdType.MESH
highest = lax.Precision.HIGHEST


def lookup(values, species):
    out = jnp.full(species.shape, values[3], jnp.float32)
    for k in range(3):
        out = jnp.where(species == k, values[k], out)
    return out


def modes_matrix(n):
    j = np.arange(n)[:, None]
    k = np.arange(n)[None, :]
    phase = 2 * np.pi * (j * k % n) / n
    m = np.where(k < n // 2, np.cos(phase), np.sin(phase)) * math.sqrt(2.0 / n)
    m = np.where(k == 0, math.sqrt(1.0 / n), m)
    m = np.where(k == n // 2, np.where(j % 2 == 0, 1, -1) * math.sqrt(1.0 / n), m)
    return m.astype(np.float32)


def mode_factors(n):
    k = np.arange(n)
    omega = 2 * np.sin(np.pi * k / n)
    gamma = np.where(k == 0, GAMMA, 2 * omega)
    c1 = np.exp(-gamma * STEP)
    c2 = np.sqrt(1 - c1 * c1)
    safe = np.where(k == 0, 1.0, omega)
    drift = np.where(k == 0, STEP, np.sin(omega * STEP) / safe)
    pull = omega * np.sin(omega * STEP)
    turn = np.cos(omega * STEP)
    out = np.zeros((n, LANES), np.float32)
    for c, v in enumerate((c1, c2, turn, drift, pull)):
        out[:, c] = v
    return out


def exchange_kernel(pos_hbm, mom_hbm, frc_hbm, noise_hbm, sp_ref, halo_ref, cos_ref, cost_ref, fac_ref,
                    pm_hbm, lo_hbm, up_hbm, hlo_ref, hup_ref,
                    raw, out_buf, in_buf, back_buf, pm_ref, load, store, send1, recv1, send2, recv2, nsend, nrecv):
    beads = in_buf.shape[0]
    me = lax.axis_index("bead")
    shard = lax.axis_index("space")
    shards = lax.axis_size("space")
    has_lower = shard > 0
    has_upper = shard < shards - 1

    loads = [pltpu.make_async_copy(src, raw.at[n], load.at[n])
             for n, src in enumerate((pos_hbm, mom_hbm, frc_hbm, noise_hbm))]
    for c in loads:
        c.start()

    barrier = pltpu.get_barrier_semaphore()

    def each(body, unroll=4):
        def run(d, _):
            body(d)
            return 0
        lax.fori_loop(1, beads, run, 0, unroll=unroll)

    each(lambda d: pl.semaphore_signal(
        barrier, inc=1, device_id={"bead": lax.rem(me + d, beads)}, device_id_type=MESH))

    @pl.when(has_lower)
    def _():
        pl.semaphore_signal(barrier, inc=1, device_id={"space": shard - 1}, device_id_type=MESH)

    @pl.when(has_upper)
    def _():
        pl.semaphore_signal(barrier, inc=1, device_id={"space": shard + 1}, device_id_type=MESH)

    for c in loads:
        c.wait()
    for c in range(3):
        s = slice(beads * c, beads * (c + 1))
        out_buf[:, c, :] = raw[0, s]
        out_buf[:, 3 + c, :] = raw[1, s] + (0.5 * STEP) * raw[2, s]
        out_buf[:, 6 + c, :] = raw[3, s]
    kinds = sp_ref[...]
    pm_ref[:, 6, :] = lookup(reach_values, kinds)
    pm_ref[:, 7, :] = lookup(strength_values, kinds)

    pl.semaphore_wait(barrier, beads - 1 + has_lower.astype(jnp.int32) + has_upper.astype(jnp.int32))

    def first(d):
        j = lax.rem(me + d, beads)
        return pltpu.make_async_remote_copy(
            src_ref=out_buf.at[j, 0:9], dst_ref=in_buf.at[me, 0:9], send_sem=send1.at[j], recv_sem=recv1.at[me],
            device_id={"bead": j}, device_id_type=MESH)

    def second(d):
        j = lax.rem(me + d, beads)
        return pltpu.make_async_remote_copy(
            src_ref=back_buf.at[j, 0:6], dst_ref=pm_ref.at[me, 0:6], send_sem=send2.at[j], recv_sem=recv2.at[me],
            device_id={"bead": j}, device_id_type=MESH)

    def arrived(buf, rows, sem, d):
        j = lax.rem(me + d, beads)
        pltpu.make_async_copy(buf.at[j, 0:rows], buf.at[j, 0:rows], sem.at[j]).wait()

    def towards(up, n):
        src, dst = ((halo_ref, hlo_ref if up else hup_ref),
                    (pm_ref.at[:, 3:8], (lo_hbm if up else up_hbm).at[:, 3:8]))[n]
        k = 2 * int(up) + n
        return pltpu.make_async_remote_copy(
            src_ref=src, dst_ref=dst, send_sem=nsend.at[k], recv_sem=nrecv.at[k],
            device_id={"space": shard + 1 if up else shard - 1}, device_id_type=MESH)

    def beside(n, act, receiving=False):
        for up, there in ((True, has_upper), (False, has_lower)):
            if receiving:
                there = has_lower if up else has_upper

            @pl.when(there)
            def _(up=up):
                act(towards(up, n))

    each(lambda d: first(d).start())
    beside(0, lambda c: c.start())
    in_buf[me] = out_buf[me]
    each(lambda d: arrived(in_buf, 9, recv1, d))

    x = jnp.concatenate([in_buf[:, r, :] for r in range(6)], axis=1)
    xi = jnp.concatenate([in_buf[:, r, :] for r in range(6, 9)], axis=1)
    modes = jnp.dot(cost_ref[...], x, precision=highest, preferred_element_type=jnp.float32)
    q, p = modes[:, 0:3 * LANES], modes[:, 3 * LANES:]
    mass = lookup(mass_values, sp_ref[pl.ds(me, 1), :])
    mass3 = jnp.concatenate([mass] * 3, axis=1)
    c1, c2, turn, drift, pull = (fac_ref[:, c:c + 1] for c in range(5))
    mixed = c1 * p + c2 * (jnp.sqrt(mass3) * xi)
    q_next = turn * q + drift * (mixed / mass3)
    p_next = turn * mixed - pull * (mass3 * q)
    beads_out = jnp.dot(cos_ref[...], jnp.concatenate([p_next, q_next], axis=1), precision=highest,
                        preferred_element_type=jnp.float32)
    for r in range(6):
        back_buf[:, r, :] = beads_out[:, LANES * r:LANES * (r + 1)]

    each(lambda d: second(d).start())
    pm_ref[me, 0:6] = back_buf[me, 0:6]
    each(lambda d: arrived(pm_ref, 6, recv2, d))

    keep = pltpu.make_async_copy(pm_ref, pm_hbm, store.at[0])
    keep.start()
    beside(1, lambda c: c.start())
    each(lambda d: first(d).wait_send())
    beside(0, lambda c: c.wait_send())
    beside(0, lambda c: c.wait_recv(), True)
    each(lambda d: second(d).wait_send())
    beside(1, lambda c: c.wait_send())
    beside(1, lambda c: c.wait_recv(), True)
    keep.wait()


def exchange(pos, mom, frc, noise, species, halo):
    beads = lax.axis_size("bead")
    chunks = species.shape[0]
    vmem = pl.BlockSpec(memory_space=pltpu.VMEM)
    hbm = pl.BlockSpec(memory_space=pl.ANY)
    f32 = jnp.float32
    block = jax.ShapeDtypeStruct((chunks, 8, LANES), f32)
    ids = jax.ShapeDtypeStruct(halo.shape, jnp.int32)
    dma = pltpu.SemaphoreType.DMA
    matrix = modes_matrix(beads)
    return pl.pallas_call(
        exchange_kernel,
        out_shape=(block, block, block, ids, ids),
        in_specs=[hbm] * 4 + [vmem] * 5,
        out_specs=(hbm,) * 3 + (vmem,) * 2,
        scratch_shapes=[
            pltpu.VMEM((4, 3 * chunks, LANES), f32),
            pltpu.VMEM((beads, 16, LANES), f32),
            pltpu.VMEM((beads, 16, LANES), f32),
            pltpu.VMEM((beads, 8, LANES), f32),
            pltpu.VMEM((chunks, 8, LANES), f32),
            dma((4,)), dma((1,)), dma((beads,)), dma((beads,)), dma((beads,)), dma((beads,)), dma((4,)), dma((4,)),
        ],
        compiler_params=pltpu.CompilerParams(collective_id=0, has_side_effects=True),
        name="exchange",
    )(pos, mom, frc, noise, species, halo, jnp.asarray(matrix), jnp.asarray(matrix.T), jnp.asarray(mode_factors(beads)))


def force_kernel(pairs_ref, count_ref, hlo_ref, hup_ref, pm_hbm, lo_hbm, up_hbm, pos_ref, mom_ref, frc_ref,
                 tab_j, tab_i, acc, pm_ref, halo, tmp, sem):
    chunks = pm_ref.shape[0]
    blocks = 2 * chunks
    left = lax.broadcasted_iota(jnp.int32, (32, LANES), 1) < 64
    left1 = left[0:8]
    get_own = pltpu.make_async_copy(pm_hbm, pm_ref, sem.at[0])
    get_own.start()
    sides = []
    shard = lax.axis_index("space")
    for side in range(2):
        there = shard > 0 if side == 0 else shard < lax.axis_size("space") - 1
        for h in range(HALO):
            b = jnp.where(there, (hup_ref if side else hlo_ref)[1 - side, h], 0)
            get = pltpu.make_async_copy((up_hbm if side else lo_hbm).at[b // 2], halo.at[side * HALO + h], sem.at[1 + side * HALO + h])
            get.start()
            sides.append((get, there, b % 2))

    def clear(i, _):
        for c in range(3):
            acc[i, c] = jnp.zeros((8, LANES), jnp.float32)
        return 0
    lax.fori_loop(0, blocks, clear, 0, unroll=8)
    tab_j[2 * HALO + blocks] = jnp.zeros(tab_j.shape[1:], jnp.float32)

    def spread(cols, e):
        for c in range(5):
            b = jnp.broadcast_to(cols[:, 3 + c:4 + c], (64, LANES))
            tab_j[e, c] = jnp.where(left, b[0:32], b[32:64])

    get_own.wait()

    def own(t, _):
        m8 = pm_ref[t]
        cols = m8.T
        spread(cols[0:64], HALO + 2 * t)
        spread(cols[64:128], HALO + 2 * t + 1)
        turned = pltpu.roll(m8, 64, 1)
        for h in range(2):
            both = jnp.where(left1, m8, turned) if h == 0 else jnp.where(left1, turned, m8)
            for c in range(4):
                tab_i[2 * t + h, c] = jnp.broadcast_to(both[3 + c:4 + c], (8, LANES))
        return 0
    lax.fori_loop(0, chunks, own, 0, unroll=8)

    for n, (get, there, half) in enumerate(sides):
        get.wait()
        tmp[n] = jnp.where(there, halo[n], 0.0).T
        cols = tmp[n, pl.ds(pl.multiple_of(half * 64, 64), 64), :]
        spread(cols, n if n < HALO else blocks + n)

    live = count_ref[0]

    def pair(p):
        i = pairs_ref[0, p]
        j = jnp.where(p < live, pairs_ref[1, p], 2 * HALO + blocks)
        xi, yi, zi, ri = (tab_i[i, c] for c in range(4))
        f = [None] * 3
        for g in range(4):
            s = pl.ds(8 * g, 8)
            dx = xi - tab_j[j, 0, s]
            dy = yi - tab_j[j, 1, s]
            dz = zi - tab_j[j, 2, s]
            d = dx * dx + dy * dy + dz * dz
            inv = 1.0 / (ri + tab_j[j, 3, s])
            w = jnp.exp(-d * inv) * (inv * tab_j[j, 4, s])
            for k, v in enumerate((dx, dy, dz)):
                f[k] = w * v if g == 0 else f[k] + w * v
        for k in range(3):
            acc[i, k] = acc[i, k] + f[k]

    def group(g, _):
        for u in range(UNROLL):
            pair(g * UNROLL + u)
        return 0
    lax.fori_loop(0, (live + UNROLL - 1) // UNROLL, group, 0)

    def finish(t, _):
        rows = pm_ref[t]
        scale = 0.02 * rows[7:8]
        for k in range(3):
            v = [jnp.sum(acc[2 * t + h, k], axis=0, keepdims=True) for h in range(2)]
            v = [x + pltpu.roll(x, 64, 1) for x in v]
            f = jnp.where(left[0:1], v[0], v[1]) * scale
            at = pl.ds(k * chunks + t, 1)
            pos_ref[at, :] = rows[3 + k:4 + k]
            frc_ref[at, :] = f
            mom_ref[at, :] = rows[k:k + 1] + 0.25 * f
        return 0
    lax.fori_loop(0, chunks, finish, 0, unroll=8)


def force_call(pairs, count, hlo, hup, pm, lo, up):
    chunks = pm.shape[0]
    smem = pl.BlockSpec(memory_space=pltpu.SMEM)
    vmem = pl.BlockSpec(memory_space=pltpu.VMEM)
    hbm = pl.BlockSpec(memory_space=pl.ANY)
    o = jax.ShapeDtypeStruct((3 * chunks, LANES), jnp.float32)
    return pl.pallas_call(
        force_kernel,
        out_shape=(o, o, o),
        in_specs=[smem] * 4 + [hbm] * 3,
        out_specs=(vmem,) * 3,
        scratch_shapes=[
            pltpu.VMEM((2 * chunks + 2 * HALO + 1, 5, 32, LANES), jnp.float32),
            pltpu.VMEM((2 * chunks, 4, 8, LANES), jnp.float32),
            pltpu.VMEM((2 * chunks, 3, 8, LANES), jnp.float32),
            pltpu.VMEM((chunks, 8, LANES), jnp.float32),
            pltpu.VMEM((2 * HALO, 8, LANES), jnp.float32),
            pltpu.VMEM((2 * HALO, LANES, 8), jnp.float32),
            pltpu.SemaphoreType.DMA((1 + 2 * HALO,)),
        ],
        compiler_params=pltpu.CompilerParams(vmem_limit_bytes=60 * 2**20),
        name="pair_forces",
    )(pairs, count, hlo, hup, pm, lo, up)


def shards(positions, momenta, forces, noise, species, block_pairs, pair_count, halo_blocks):
    flat = [a.reshape(-1, LANES) for a in (positions, momenta, forces, noise)]
    pm, lo, up, hlo, hup = exchange(*flat, species.reshape(-1, LANES), halo_blocks)
    outs = force_call(block_pairs, pair_count, hlo, hup, pm, lo, up)
    return tuple(o.reshape(positions.shape) for o in outs)


def solution(mesh):
    big = P("bead", None, "space")
    in_specs = (big, big, big, big, P("space"), P(None, "space"), P("space"), P(None, "space"))
    return jax.shard_map(shards, mesh=mesh, in_specs=in_specs, out_specs=(big, big, big), check_vma=False)
```

time: 73 us -> 58.6 us (0.80)
  the two profiles are of different devices: /device:TPU:24 before, /device:TPU:32 now
where the time goes in v1:
time: 58.6 us; the launch traced here: 58.3 us
  Pallas kernels  57 us (97%)
  between operations  1.29 us (2%)
    pallas_call x1, Pallas kernels, exchange(): pl.pallas_call(exchange_kernel, out_shape=(block, block, block, ids, ids)...  31.4 us
    pallas_call x1, Pallas kernels, force_call(): pl.pallas_call(force_kernel, out_shape=(o, o, o), in_specs=[smem] * 4 + [...  25.6 us

profile of v1, /device:TPU:32, one launch (start us, length us, event | category | flops | bytes accessed | tf_op | source)
XLA Modules:
  0.0 58.3 jit_solution(17071223835094152099)
XLA Ops:
  1.3 31.4 %exchange.1 = (f32[32,8,128]{2,1,0:T(8,128)}, f32[32,8,128]{2,1,0:T(8,128)}, f32[32,8,128]{2,1,0:T(8,128)}, s32[2,4]{1,0:T(2,128)}, s32[2,4]{1,0:T(2,128)}) custom-call(f32[96,128]{1,0:T(8,128)} %bitcast.8, f32[96,128]{1,0:T(8,128)} %bitcast.9, f32[96,128]{1,0:T(8,128)} %bitcast.10, f32[96,128]{1,0:T(8,128)} %bitcast.11, s32[32,128]{1,0:T(8,128)} %bitcast.12, ...), custom_call_target="tpu_custom_call" | custom-call | tf_op jit(solution)/shard_map/exchange/pallas_call | solution.py:184
  32.7 25.6 %pair_forces.1 = (f32[96,128]{1,0:T(8,128)}, f32[96,128]{1,0:T(8,128)}, f32[96,128]{1,0:T(8,128)}) custom-call(s32[2,1024]{1,0:T(2,128)} %pairs_ref.1, s32[1]{0:T(128)S(6)} %copy.20.count_ref, s32[2,4]{1,0:T(2,128)} %get-tuple-element.11.hlo_ref, s32[2,4]{1,0:T(2,128)} %get-tuple-element.12.hup_ref, f32[32,8,128]{2,1,0:T(8,128)} %get-tuple-element.13.pm_hbm, ...), custom_call_target="tpu_custom_call" | custom-call | tf_op jit(solution)/shard_map/pair_forces/pallas_call | solution.py:300

commit v2 on v1

--- a/solution.py
+++ b/solution.py
@@ -12,7 +12,8 @@
 BLOCK = 64
 LANES = 128
 HALO = 4
-UNROLL = 4
+UNROLL = 16
+ROOT = math.sqrt(math.log2(math.e))
 STEP = 0.5
 GAMMA = 0.5
 mass_values = (1.0, 0.3, 2.5, 0.75)
@@ -58,7 +59,7 @@
 def exchange_kernel(pos_hbm, mom_hbm, frc_hbm, noise_hbm, sp_ref, halo_ref, cos_ref, cost_ref, fac_ref,
                     pm_hbm, lo_hbm, up_hbm, hlo_ref, hup_ref,
                     raw, out_buf, in_buf, back_buf, pm_ref, load, store, send1, recv1, send2, recv2, nsend, nrecv):
-    beads = in_buf.shape[0]
+    beads = lax.axis_size("bead")
     me = lax.axis_index("bead")
     shard = lax.axis_index("space")
     shards = lax.axis_size("space")
@@ -93,9 +94,9 @@
         c.wait()
     for c in range(3):
         s = slice(beads * c, beads * (c + 1))
-        out_buf[:, c, :] = raw[0, s]
-        out_buf[:, 3 + c, :] = raw[1, s] + (0.5 * STEP) * raw[2, s]
-        out_buf[:, 6 + c, :] = raw[3, s]
+        out_buf[pl.ds(c, beads, stride=9), :] = raw[0, s]
+        out_buf[pl.ds(3 + c, beads, stride=9), :] = raw[1, s] + (0.5 * STEP) * raw[2, s]
+        out_buf[pl.ds(6 + c, beads, stride=9), :] = raw[3, s]
     kinds = sp_ref[...]
     pm_ref[:, 6, :] = lookup(reach_values, kinds)
     pm_ref[:, 7, :] = lookup(strength_values, kinds)
@@ -105,18 +106,22 @@
     def first(d):
         j = lax.rem(me + d, beads)
         return pltpu.make_async_remote_copy(
-            src_ref=out_buf.at[j, 0:9], dst_ref=in_buf.at[me, 0:9], send_sem=send1.at[j], recv_sem=recv1.at[me],
+            src_ref=out_buf.at[pl.ds(9 * j, 9)], dst_ref=in_buf.at[pl.ds(9 * me, 9)], send_sem=send1, recv_sem=recv1,
             device_id={"bead": j}, device_id_type=MESH)
 
     def second(d):
         j = lax.rem(me + d, beads)
         return pltpu.make_async_remote_copy(
-            src_ref=back_buf.at[j, 0:6], dst_ref=pm_ref.at[me, 0:6], send_sem=send2.at[j], recv_sem=recv2.at[me],
+            src_ref=back_buf.at[j, 0:6], dst_ref=pm_ref.at[me, 0:6], send_sem=send2, recv_sem=recv2,
             device_id={"bead": j}, device_id_type=MESH)
 
-    def arrived(buf, rows, sem, d):
-        j = lax.rem(me + d, beads)
-        pltpu.make_async_copy(buf.at[j, 0:rows], buf.at[j, 0:rows], sem.at[j]).wait()
+    def all_of(buf, rows, sem):
+        part = buf.at[0:beads - 1, 0:rows]
+        pltpu.make_async_copy(part, part, sem).wait()
+
+    def all_rows(buf, rows, sem):
+        part = buf.at[0:rows * (beads - 1)]
+        pltpu.make_async_copy(part, part, sem).wait()
 
     def towards(up, n):
         src, dst = ((halo_ref, hlo_ref if up else hup_ref),
@@ -137,11 +142,11 @@
 
     each(lambda d: first(d).start())
     beside(0, lambda c: c.start())
-    in_buf[me] = out_buf[me]
-    each(lambda d: arrived(in_buf, 9, recv1, d))
-
-    x = jnp.concatenate([in_buf[:, r, :] for r in range(6)], axis=1)
-    xi = jnp.concatenate([in_buf[:, r, :] for r in range(6, 9)], axis=1)
+    in_buf[pl.ds(9 * me, 9), :] = out_buf[pl.ds(9 * me, 9), :]
+    all_rows(in_buf, 9, recv1)
+
+    x = jnp.concatenate([in_buf[pl.ds(r, beads, stride=9), :] for r in range(6)], axis=1)
+    xi = jnp.concatenate([in_buf[pl.ds(r, beads, stride=9), :] for r in range(6, 9)], axis=1)
     modes = jnp.dot(cost_ref[...], x, precision=highest, preferred_element_type=jnp.float32)
     q, p = modes[:, 0:3 * LANES], modes[:, 3 * LANES:]
     mass = lookup(mass_values, sp_ref[pl.ds(me, 1), :])
@@ -157,15 +162,15 @@
 
     each(lambda d: second(d).start())
     pm_ref[me, 0:6] = back_buf[me, 0:6]
-    each(lambda d: arrived(pm_ref, 6, recv2, d))
+    all_of(pm_ref, 6, recv2)
 
     keep = pltpu.make_async_copy(pm_ref, pm_hbm, store.at[0])
     keep.start()
     beside(1, lambda c: c.start())
-    each(lambda d: first(d).wait_send())
+    all_rows(out_buf, 9, send1)
     beside(0, lambda c: c.wait_send())
     beside(0, lambda c: c.wait_recv(), True)
-    each(lambda d: second(d).wait_send())
+    all_of(back_buf, 6, send2)
     beside(1, lambda c: c.wait_send())
     beside(1, lambda c: c.wait_recv(), True)
     keep.wait()
@@ -188,11 +193,11 @@
         out_specs=(hbm,) * 3 + (vmem,) * 2,
         scratch_shapes=[
             pltpu.VMEM((4, 3 * chunks, LANES), f32),
-            pltpu.VMEM((beads, 16, LANES), f32),
-            pltpu.VMEM((beads, 16, LANES), f32),
+            pltpu.VMEM((beads * 9, LANES), f32),
+            pltpu.VMEM((beads * 9, LANES), f32),
             pltpu.VMEM((beads, 8, LANES), f32),
             pltpu.VMEM((chunks, 8, LANES), f32),
-            dma((4,)), dma((1,)), dma((beads,)), dma((beads,)), dma((beads,)), dma((beads,)), dma((4,)), dma((4,)),
+            dma((4,)), dma((1,)), dma, dma, dma, dma, dma((4,)), dma((4,)),
         ],
         compiler_params=pltpu.CompilerParams(collective_id=0, has_side_effects=True),
         name="exchange",
@@ -200,7 +205,7 @@
 
 
 def force_kernel(pairs_ref, count_ref, hlo_ref, hup_ref, pm_hbm, lo_hbm, up_hbm, pos_ref, mom_ref, frc_ref,
-                 tab_j, tab_i, acc, pm_ref, halo, tmp, sem):
+                 tab_j, tab_i, acc, pm_ref, halo, sem):
     chunks = pm_ref.shape[0]
     blocks = 2 * chunks
     left = lax.broadcasted_iota(jnp.int32, (32, LANES), 1) < 64
@@ -218,24 +223,42 @@
             sides.append((get, there, b % 2))
 
     def clear(i, _):
-        for c in range(3):
-            acc[i, c] = jnp.zeros((8, LANES), jnp.float32)
+        acc[i] = jnp.zeros((24, LANES), jnp.float32)
         return 0
     lax.fori_loop(0, blocks, clear, 0, unroll=8)
     tab_j[2 * HALO + blocks] = jnp.zeros(tab_j.shape[1:], jnp.float32)
 
-    def spread(cols, e):
-        for c in range(5):
-            b = jnp.broadcast_to(cols[:, 3 + c:4 + c], (64, LANES))
-            tab_j[e, c] = jnp.where(left, b[0:32], b[32:64])
+    row = lax.broadcasted_iota(jnp.int32, (32, LANES), 0)
+    lane = lax.broadcasted_iota(jnp.int32, (32, LANES), 1)
+    picks = [(lane == 64 * h + row) | (lane == 64 * h + 32 + row) for h in range(2)]
+    k = lax.broadcasted_iota(jnp.int32, (2 * LANES, LANES), 0)
+    n = lax.broadcasted_iota(jnp.int32, (2 * LANES, LANES), 1)
+    halves = ((k % 64 < 32) == (n < 64)).astype(jnp.bfloat16)
+    kind = lax.broadcasted_iota(jnp.int32, (8, LANES), 0)
+    factor = jnp.where(kind < 3, 1.0, jnp.where(kind < 6, ROOT, jnp.where(kind == 6, -1.0, 1.0)))
+
+    def parts(m8):
+        high = m8.astype(jnp.bfloat16).astype(jnp.float32)
+        rest = m8 - high
+        mid = rest.astype(jnp.bfloat16).astype(jnp.float32)
+        return high, mid, rest - mid
+
+    def spread_mxu(m8, hs):
+        ps = parts(m8)
+        lhs = [jnp.concatenate([jnp.where(picks[h], p[3 + c:4 + c], 0.0) for h in hs for c in range(5)], axis=0).astype(jnp.bfloat16) for p in ps]
+        both = jnp.concatenate([lhs[0], lhs[1]], axis=1)
+        out = jnp.dot(both, halves, preferred_element_type=jnp.float32)
+        return out + jnp.dot(lhs[2], halves[0:LANES], preferred_element_type=jnp.float32)
 
     get_own.wait()
 
     def own(t, _):
-        m8 = pm_ref[t]
-        cols = m8.T
-        spread(cols[0:64], HALO + 2 * t)
-        spread(cols[64:128], HALO + 2 * t + 1)
+        m8 = pm_ref[t] * factor
+        out = spread_mxu(m8, (0, 1))
+        for h in range(2):
+            for c in range(5):
+                s = 160 * h + 32 * c
+                tab_j[HALO + 2 * t + h, c] = out[s:s + 32]
         turned = pltpu.roll(m8, 64, 1)
         for h in range(2):
             both = jnp.where(left1, m8, turned) if h == 0 else jnp.where(left1, turned, m8)
@@ -244,11 +267,15 @@
         return 0
     lax.fori_loop(0, chunks, own, 0, unroll=8)
 
-    for n, (get, there, half) in enumerate(sides):
+    for get, _, _ in sides:
         get.wait()
-        tmp[n] = jnp.where(there, halo[n], 0.0).T
-        cols = tmp[n, pl.ds(pl.multiple_of(half * 64, 64), 64), :]
-        spread(cols, n if n < HALO else blocks + n)
+    for n_, (get, there, half) in enumerate(sides):
+        e = n_ if n_ < HALO else blocks + n_
+        m8 = jnp.where(there, halo[n_], 0.0) * factor
+        m8 = jnp.where(half == 1, pltpu.roll(m8, 64, 1), m8)
+        out = spread_mxu(m8, (0,))
+        for c in range(5):
+            tab_j[e, c] = out[32 * c:32 * c + 32]
 
     live = count_ref[0]
 
@@ -264,23 +291,24 @@
             dz = zi - tab_j[j, 2, s]
             d = dx * dx + dy * dy + dz * dz
             inv = 1.0 / (ri + tab_j[j, 3, s])
-            w = jnp.exp(-d * inv) * (inv * tab_j[j, 4, s])
+            w = jnp.exp2(d * inv) * (inv * tab_j[j, 4, s])
             for k, v in enumerate((dx, dy, dz)):
                 f[k] = w * v if g == 0 else f[k] + w * v
-        for k in range(3):
-            acc[i, k] = acc[i, k] + f[k]
+        return i, f
 
     def group(g, _):
         for u in range(UNROLL):
-            pair(g * UNROLL + u)
+            i, f = pair(g * UNROLL + u)
+            for k in range(3):
+                acc[i, pl.ds(8 * k, 8)] = acc[i, pl.ds(8 * k, 8)] + f[k]
         return 0
     lax.fori_loop(0, (live + UNROLL - 1) // UNROLL, group, 0)
 
     def finish(t, _):
         rows = pm_ref[t]
-        scale = 0.02 * rows[7:8]
+        scale = (-0.02 / ROOT) * rows[7:8]
         for k in range(3):
-            v = [jnp.sum(acc[2 * t + h, k], axis=0, keepdims=True) for h in range(2)]
+            v = [jnp.sum(acc[2 * t + h, pl.ds(8 * k, 8)], axis=0, keepdims=True) for h in range(2)]
             v = [x + pltpu.roll(x, 64, 1) for x in v]
             f = jnp.where(left[0:1], v[0], v[1]) * scale
             at = pl.ds(k * chunks + t, 1)
@@ -305,10 +333,9 @@
         scratch_shapes=[
             pltpu.VMEM((2 * chunks + 2 * HALO + 1, 5, 32, LANES), jnp.float32),
             pltpu.VMEM((2 * chunks, 4, 8, LANES), jnp.float32),
-            pltpu.VMEM((2 * chunks, 3, 8, LANES), jnp.float32),
+            pltpu.VMEM((2 * chunks, 24, LANES), jnp.float32),
             pltpu.VMEM((chunks, 8, LANES), jnp.float32),
             pltpu.VMEM((2 * HALO, 8, LANES), jnp.float32),
-            pltpu.VMEM((2 * HALO, LANES, 8), jnp.float32),
             pltpu.SemaphoreType.DMA((1 + 2 * HALO,)),
         ],
         compiler_params=pltpu.CompilerParams(vmem_limit_bytes=60 * 2**20),

time: 58.6 us -> 49.9 us (0.85)
  the two profiles are of different devices: /device:TPU:32 before, /device:TPU:16 now
where the time goes in v2:
time: 49.9 us; the launch traced here: 49.6 us
  Pallas kernels  48.3 us (97%)
  between operations  1.29 us (3%)
    pallas_call x1, Pallas kernels, exchange(): pl.pallas_call(exchange_kernel, out_shape=(block, block, block, ids, ids)...  30.2 us
    pallas_call x1, Pallas kernels, force_call(): pl.pallas_call(force_kernel, out_shape=(o, o, o), in_specs=[smem] * 4 + [...  18.1 us

profile of v2, /device:TPU:16, one launch (start us, length us, event | category | flops | bytes accessed | tf_op | source)
XLA Modules:
  0.0 49.6 jit_solution(17680516046252764192)
XLA Ops:
  1.3 30.2 %exchange.1 = (f32[32,8,128]{2,1,0:T(8,128)}, f32[32,8,128]{2,1,0:T(8,128)}, f32[32,8,128]{2,1,0:T(8,128)}, s32[2,4]{1,0:T(2,128)}, s32[2,4]{1,0:T(2,128)}) custom-call(f32[96,128]{1,0:T(8,128)} %bitcast.8, f32[96,128]{1,0:T(8,128)} %bitcast.9, f32[96,128]{1,0:T(8,128)} %bitcast.10, f32[96,128]{1,0:T(8,128)} %bitcast.11, s32[32,128]{1,0:T(8,128)} %bitcast.12, ...), custom_call_target="tpu_custom_call" | custom-call | tf_op jit(solution)/shard_map/exchange/pallas_call | solution.py:189
  31.5 18.1 %pair_forces.1 = (f32[96,128]{1,0:T(8,128)}, f32[96,128]{1,0:T(8,128)}, f32[96,128]{1,0:T(8,128)}) custom-call(s32[2,1024]{1,0:T(2,128)} %pairs_ref.1, s32[1]{0:T(128)S(6)} %copy.20.count_ref, s32[2,4]{1,0:T(2,128)} %get-tuple-element.11.hlo_ref, s32[2,4]{1,0:T(2,128)} %get-tuple-element.12.hup_ref, f32[32,8,128]{2,1,0:T(8,128)} %get-tuple-element.13.pm_hbm, ...), custom_call_target="tpu_custom_call" | custom-call | tf_op jit(solution)/shard_map/pair_forces/pallas_call | solution.py:328

commit v3 on v2

--- a/solution.py
+++ b/solution.py
@@ -12,7 +12,7 @@
 BLOCK = 64
 LANES = 128
 HALO = 4
-UNROLL = 16
+UNROLL = 64
 ROOT = math.sqrt(math.log2(math.e))
 STEP = 0.5
 GAMMA = 0.5
@@ -73,22 +73,20 @@
 
     barrier = pltpu.get_barrier_semaphore()
 
-    def each(body, unroll=4):
+    def each(body, first=1, unroll=4):
         def run(d, _):
             body(d)
             return 0
-        lax.fori_loop(1, beads, run, 0, unroll=unroll)
+        lax.fori_loop(first, beads, run, 0, unroll=unroll)
 
     each(lambda d: pl.semaphore_signal(
         barrier, inc=1, device_id={"bead": lax.rem(me + d, beads)}, device_id_type=MESH))
 
-    @pl.when(has_lower)
-    def _():
-        pl.semaphore_signal(barrier, inc=1, device_id={"space": shard - 1}, device_id_type=MESH)
-
-    @pl.when(has_upper)
-    def _():
-        pl.semaphore_signal(barrier, inc=1, device_id={"space": shard + 1}, device_id_type=MESH)
+    for there, other in ((has_lower, shard - 1), (has_upper, shard + 1)):
+        @pl.when(there)
+        def _(other=other):
+            each(lambda d: pl.semaphore_signal(
+                barrier, inc=1, device_id={"bead": lax.rem(me + d, beads), "space": other}, device_id_type=MESH), 0)
 
     for c in loads:
         c.wait()
@@ -101,7 +99,7 @@
     pm_ref[:, 6, :] = lookup(reach_values, kinds)
     pm_ref[:, 7, :] = lookup(strength_values, kinds)
 
-    pl.semaphore_wait(barrier, beads - 1 + has_lower.astype(jnp.int32) + has_upper.astype(jnp.int32))
+    pl.semaphore_wait(barrier, beads - 1 + beads * (has_lower.astype(jnp.int32) + has_upper.astype(jnp.int32)))
 
     def first(d):
         j = lax.rem(me + d, beads)
@@ -123,25 +121,38 @@
         part = buf.at[0:rows * (beads - 1)]
         pltpu.make_async_copy(part, part, sem).wait()
 
-    def towards(up, n):
-        src, dst = ((halo_ref, hlo_ref if up else hup_ref),
-                    (pm_ref.at[:, 3:8], (lo_hbm if up else up_hbm).at[:, 3:8]))[n]
-        k = 2 * int(up) + n
-        return pltpu.make_async_remote_copy(
-            src_ref=src, dst_ref=dst, send_sem=nsend.at[k], recv_sem=nrecv.at[k],
-            device_id={"space": shard + 1 if up else shard - 1}, device_id_type=MESH)
-
-    def beside(n, act, receiving=False):
+    def lists(up):
+        return pltpu.make_async_remote_copy(
+            src_ref=halo_ref, dst_ref=hlo_ref if up else hup_ref, send_sem=nsend.at[int(up)],
+            recv_sem=nrecv.at[int(up)], device_id={"space": shard + 1 if up else shard - 1}, device_id_type=MESH)
+
+    def bounds(up):
+        return pltpu.make_async_remote_copy(
+            src_ref=pm_ref.at[:, 6:8], dst_ref=(lo_hbm if up else up_hbm).at[:, 6:8], send_sem=nsend.at[4 + int(up)],
+            recv_sem=nrecv.at[4 + int(up)], device_id={"space": shard + 1 if up else shard - 1}, device_id_type=MESH)
+
+    def beyond(up, d):
+        j = lax.rem(me + d, beads)
+        return pltpu.make_async_remote_copy(
+            src_ref=back_buf.at[j, 3:6], dst_ref=(lo_hbm if up else up_hbm).at[me, 3:6],
+            send_sem=nsend.at[2 + int(up)], recv_sem=nrecv.at[2 + int(up)],
+            device_id={"bead": j, "space": shard + 1 if up else shard - 1}, device_id_type=MESH)
+
+    def beside(act, receiving=False):
         for up, there in ((True, has_upper), (False, has_lower)):
             if receiving:
                 there = has_lower if up else has_upper
 
             @pl.when(there)
             def _(up=up):
-                act(towards(up, n))
+                act(up)
+
+    def all_beyond(buf, sem):
+        part = buf.at[:, 3:6]
+        pltpu.make_async_copy(part, part, sem).wait()
 
     each(lambda d: first(d).start())
-    beside(0, lambda c: c.start())
+    beside(lambda up: (lists(up).start(), bounds(up).start()))
     in_buf[pl.ds(9 * me, 9), :] = out_buf[pl.ds(9 * me, 9), :]
     all_rows(in_buf, 9, recv1)
 
@@ -161,18 +172,18 @@
         back_buf[:, r, :] = beads_out[:, LANES * r:LANES * (r + 1)]
 
     each(lambda d: second(d).start())
+    beside(lambda up: each(lambda d: beyond(up, d).start(), 0))
     pm_ref[me, 0:6] = back_buf[me, 0:6]
     all_of(pm_ref, 6, recv2)
 
     keep = pltpu.make_async_copy(pm_ref, pm_hbm, store.at[0])
     keep.start()
-    beside(1, lambda c: c.start())
     all_rows(out_buf, 9, send1)
-    beside(0, lambda c: c.wait_send())
-    beside(0, lambda c: c.wait_recv(), True)
+    beside(lambda up: (lists(up).wait_send(), bounds(up).wait_send()))
+    beside(lambda up: (lists(up).wait_recv(), bounds(up).wait_recv()), True)
     all_of(back_buf, 6, send2)
-    beside(1, lambda c: c.wait_send())
-    beside(1, lambda c: c.wait_recv(), True)
+    beside(lambda up: all_beyond(back_buf, nsend.at[2 + int(up)]))
+    beside(lambda up: all_beyond(lo_hbm if up else up_hbm, nrecv.at[2 + int(up)]), True)
     keep.wait()
 
 
@@ -197,7 +208,7 @@
             pltpu.VMEM((beads * 9, LANES), f32),
             pltpu.VMEM((beads, 8, LANES), f32),
             pltpu.VMEM((chunks, 8, LANES), f32),
-            dma((4,)), dma((1,)), dma, dma, dma, dma, dma((4,)), dma((4,)),
+            dma((4,)), dma((1,)), dma, dma, dma, dma, dma((6,)), dma((6,)),
         ],
         compiler_params=pltpu.CompilerParams(collective_id=0, has_side_effects=True),
         name="exchange",
@@ -265,7 +276,7 @@
             for c in range(4):
                 tab_i[2 * t + h, c] = jnp.broadcast_to(both[3 + c:4 + c], (8, LANES))
         return 0
-    lax.fori_loop(0, chunks, own, 0, unroll=8)
+    lax.fori_loop(0, chunks, own, 0, unroll=16)
 
     for get, _, _ in sides:
         get.wait()

time: 49.9 us -> 50.2 us (level)
  the two profiles are of different devices: /device:TPU:16 before, /device:TPU:41 now
where the time goes in v3:
time: 50.2 us; the launch traced here: 49.9 us
  Pallas kernels  48.6 us (97%)
  between operations  1.29 us (3%)
    pallas_call x1, Pallas kernels, exchange(): pl.pallas_call(exchange_kernel, out_shape=(block, block, block, ids, ids)...  31.4 us
    pallas_call x1, Pallas kernels, force_call(): pl.pallas_call(force_kernel, out_shape=(o, o, o), in_specs=[smem] * 4 + [...  17.2 us

profile of v3, /device:TPU:41, one launch (start us, length us, event | category | flops | bytes accessed | tf_op | source)
XLA Modules:
  0.0 49.9 jit_solution(3904049219064566908)
XLA Ops:
  1.3 31.4 %exchange.1 = (f32[32,8,128]{2,1,0:T(8,128)}, f32[32,8,128]{2,1,0:T(8,128)}, f32[32,8,128]{2,1,0:T(8,128)}, s32[2,4]{1,0:T(2,128)}, s32[2,4]{1,0:T(2,128)}) custom-call(f32[96,128]{1,0:T(8,128)} %bitcast.8, f32[96,128]{1,0:T(8,128)} %bitcast.9, f32[96,128]{1,0:T(8,128)} %bitcast.10, f32[96,128]{1,0:T(8,128)} %bitcast.11, s32[32,128]{1,0:T(8,128)} %bitcast.12, ...), custom_call_target="tpu_custom_call" | custom-call | tf_op jit(solution)/shard_map/exchange/pallas_call | solution.py:200
  32.7 17.2 %pair_forces.1 = (f32[96,128]{1,0:T(8,128)}, f32[96,128]{1,0:T(8,128)}, f32[96,128]{1,0:T(8,128)}) custom-call(s32[2,1024]{1,0:T(2,128)} %pairs_ref.1, s32[1]{0:T(128)S(6)} %copy.20.count_ref, s32[2,4]{1,0:T(2,128)} %get-tuple-element.11.hlo_ref, s32[2,4]{1,0:T(2,128)} %get-tuple-element.12.hup_ref, f32[32,8,128]{2,1,0:T(8,128)} %get-tuple-element.13.pm_hbm, ...), custom_call_target="tpu_custom_call" | custom-call | tf_op jit(solution)/shard_map/pair_forces/pallas_call | solution.py:339

commit v4 on v3

--- a/solution.py
+++ b/solution.py
@@ -56,9 +56,9 @@
     return out
 
 
-def exchange_kernel(pos_hbm, mom_hbm, frc_hbm, noise_hbm, sp_ref, halo_ref, cos_ref, cost_ref, fac_ref,
-                    pm_hbm, lo_hbm, up_hbm, hlo_ref, hup_ref,
-                    raw, out_buf, in_buf, back_buf, pm_ref, load, store, send1, recv1, send2, recv2, nsend, nrecv):
+def exchange_kernel(pos_hbm, mom_hbm, frc_hbm, noise_hbm, sp_hbm, halo_hbm, fixed_hbm,
+                    pm_hbm, lo_hbm, up_hbm, hlo_hbm, hup_hbm,
+                    raw, sp_ref, fixed, out_buf, in_buf, back_buf, range_buf, load, store, send1, recv1, send2, recv2, nsend, nrecv):
     beads = lax.axis_size("bead")
     me = lax.axis_index("bead")
     shard = lax.axis_index("space")
@@ -66,11 +66,6 @@
     has_lower = shard > 0
     has_upper = shard < shards - 1
 
-    loads = [pltpu.make_async_copy(src, raw.at[n], load.at[n])
-             for n, src in enumerate((pos_hbm, mom_hbm, frc_hbm, noise_hbm))]
-    for c in loads:
-        c.start()
-
     barrier = pltpu.get_barrier_semaphore()
 
     def each(body, first=1, unroll=4):
@@ -88,6 +83,11 @@
             each(lambda d: pl.semaphore_signal(
                 barrier, inc=1, device_id={"bead": lax.rem(me + d, beads), "space": other}, device_id_type=MESH), 0)
 
+    loads = [pltpu.make_async_copy(src, dst, load.at[n]) for n, (src, dst) in enumerate((
+        (pos_hbm, raw.at[0]), (mom_hbm, raw.at[1]), (frc_hbm, raw.at[2]), (noise_hbm, raw.at[3]),
+        (sp_hbm, sp_ref), (fixed_hbm, fixed)))]
+    for c in loads:
+        c.start()
     for c in loads:
         c.wait()
     for c in range(3):
@@ -96,8 +96,10 @@
         out_buf[pl.ds(3 + c, beads, stride=9), :] = raw[1, s] + (0.5 * STEP) * raw[2, s]
         out_buf[pl.ds(6 + c, beads, stride=9), :] = raw[3, s]
     kinds = sp_ref[...]
-    pm_ref[:, 6, :] = lookup(reach_values, kinds)
-    pm_ref[:, 7, :] = lookup(strength_values, kinds)
+    range_buf[:, 0, :] = lookup(reach_values, kinds)
+    range_buf[:, 1, :] = lookup(strength_values, kinds)
+    keep = pltpu.make_async_copy(range_buf, pm_hbm.at[:, 6:8], store.at[0])
+    keep.start()
 
     pl.semaphore_wait(barrier, beads - 1 + beads * (has_lower.astype(jnp.int32) + has_upper.astype(jnp.int32)))
 
@@ -110,7 +112,7 @@
     def second(d):
         j = lax.rem(me + d, beads)
         return pltpu.make_async_remote_copy(
-            src_ref=back_buf.at[j, 0:6], dst_ref=pm_ref.at[me, 0:6], send_sem=send2, recv_sem=recv2,
+            src_ref=back_buf.at[j, 0:6], dst_ref=pm_hbm.at[me, 0:6], send_sem=send2, recv_sem=recv2,
             device_id={"bead": j}, device_id_type=MESH)
 
     def all_of(buf, rows, sem):
@@ -123,12 +125,12 @@
 
     def lists(up):
         return pltpu.make_async_remote_copy(
-            src_ref=halo_ref, dst_ref=hlo_ref if up else hup_ref, send_sem=nsend.at[int(up)],
+            src_ref=halo_hbm, dst_ref=hlo_hbm if up else hup_hbm, send_sem=nsend.at[int(up)],
             recv_sem=nrecv.at[int(up)], device_id={"space": shard + 1 if up else shard - 1}, device_id_type=MESH)
 
     def bounds(up):
         return pltpu.make_async_remote_copy(
-            src_ref=pm_ref.at[:, 6:8], dst_ref=(lo_hbm if up else up_hbm).at[:, 6:8], send_sem=nsend.at[4 + int(up)],
+            src_ref=range_buf, dst_ref=(lo_hbm if up else up_hbm).at[:, 6:8], send_sem=nsend.at[4 + int(up)],
             recv_sem=nrecv.at[4 + int(up)], device_id={"space": shard + 1 if up else shard - 1}, device_id_type=MESH)
 
     def beyond(up, d):
@@ -158,26 +160,26 @@
 
     x = jnp.concatenate([in_buf[pl.ds(r, beads, stride=9), :] for r in range(6)], axis=1)
     xi = jnp.concatenate([in_buf[pl.ds(r, beads, stride=9), :] for r in range(6, 9)], axis=1)
-    modes = jnp.dot(cost_ref[...], x, precision=highest, preferred_element_type=jnp.float32)
+    modes = jnp.dot(fixed[beads:2 * beads, 0:beads], x, precision=highest, preferred_element_type=jnp.float32)
     q, p = modes[:, 0:3 * LANES], modes[:, 3 * LANES:]
     mass = lookup(mass_values, sp_ref[pl.ds(me, 1), :])
     mass3 = jnp.concatenate([mass] * 3, axis=1)
-    c1, c2, turn, drift, pull = (fac_ref[:, c:c + 1] for c in range(5))
+    c1, c2, turn, drift, pull = (fixed[2 * beads:3 * beads, c:c + 1] for c in range(5))
     mixed = c1 * p + c2 * (jnp.sqrt(mass3) * xi)
     q_next = turn * q + drift * (mixed / mass3)
     p_next = turn * mixed - pull * (mass3 * q)
-    beads_out = jnp.dot(cos_ref[...], jnp.concatenate([p_next, q_next], axis=1), precision=highest,
+    beads_out = jnp.dot(fixed[0:beads, 0:beads], jnp.concatenate([p_next, q_next], axis=1), precision=highest,
                         preferred_element_type=jnp.float32)
     for r in range(6):
         back_buf[:, r, :] = beads_out[:, LANES * r:LANES * (r + 1)]
 
     each(lambda d: second(d).start())
     beside(lambda up: each(lambda d: beyond(up, d).start(), 0))
-    pm_ref[me, 0:6] = back_buf[me, 0:6]
-    all_of(pm_ref, 6, recv2)
-
-    keep = pltpu.make_async_copy(pm_ref, pm_hbm, store.at[0])
-    keep.start()
+    own = pltpu.make_async_copy(back_buf.at[me, 0:6], pm_hbm.at[me, 0:6], store.at[1])
+    own.start()
+    all_of(pm_hbm, 6, recv2)
+    own.wait()
+
     all_rows(out_buf, 9, send1)
     beside(lambda up: (lists(up).wait_send(), bounds(up).wait_send()))
     beside(lambda up: (lists(up).wait_recv(), bounds(up).wait_recv()), True)
@@ -190,29 +192,33 @@
 def exchange(pos, mom, frc, noise, species, halo):
     beads = lax.axis_size("bead")
     chunks = species.shape[0]
-    vmem = pl.BlockSpec(memory_space=pltpu.VMEM)
     hbm = pl.BlockSpec(memory_space=pl.ANY)
     f32 = jnp.float32
     block = jax.ShapeDtypeStruct((chunks, 8, LANES), f32)
     ids = jax.ShapeDtypeStruct(halo.shape, jnp.int32)
     dma = pltpu.SemaphoreType.DMA
-    matrix = modes_matrix(beads)
+    fixed = np.zeros((3, beads, LANES), np.float32)
+    fixed[0, :, 0:beads] = modes_matrix(beads)
+    fixed[1, :, 0:beads] = modes_matrix(beads).T
+    fixed[2] = mode_factors(beads)
     return pl.pallas_call(
         exchange_kernel,
         out_shape=(block, block, block, ids, ids),
-        in_specs=[hbm] * 4 + [vmem] * 5,
-        out_specs=(hbm,) * 3 + (vmem,) * 2,
+        in_specs=[hbm] * 7,
+        out_specs=(hbm,) * 5,
         scratch_shapes=[
             pltpu.VMEM((4, 3 * chunks, LANES), f32),
+            pltpu.VMEM((chunks, LANES), jnp.int32),
+            pltpu.VMEM((3 * beads, LANES), f32),
             pltpu.VMEM((beads * 9, LANES), f32),
             pltpu.VMEM((beads * 9, LANES), f32),
             pltpu.VMEM((beads, 8, LANES), f32),
-            pltpu.VMEM((chunks, 8, LANES), f32),
-            dma((4,)), dma((1,)), dma, dma, dma, dma, dma((6,)), dma((6,)),
+            pltpu.VMEM((chunks, 2, LANES), f32),
+            dma((6,)), dma((2,)), dma, dma, dma, dma, dma((6,)), dma((6,)),
         ],
         compiler_params=pltpu.CompilerParams(collective_id=0, has_side_effects=True),
         name="exchange",
-    )(pos, mom, frc, noise, species, halo, jnp.asarray(matrix), jnp.asarray(matrix.T), jnp.asarray(mode_factors(beads)))
+    )(pos, mom, frc, noise, species, halo, jnp.asarray(fixed.reshape(3 * beads, LANES)))
 
 
 def force_kernel(pairs_ref, count_ref, hlo_ref, hup_ref, pm_hbm, lo_hbm, up_hbm, pos_ref, mom_ref, frc_ref,

time: 50.2 us -> 47.3 us (0.942)
  the two profiles are of different devices: /device:TPU:41 before, /device:TPU:56 now
where the time goes in v4:
time: 47.3 us; the launch traced here: 47 us
  Pallas kernels  45.8 us (97%)
  between operations  1.29 us (3%)
    pallas_call x1, Pallas kernels, exchange(): pl.pallas_call(exchange_kernel, out_shape=(block, block, block, ids, ids)...  28.6 us
    pallas_call x1, Pallas kernels, force_call(): pl.pallas_call(force_kernel, out_shape=(o, o, o), in_specs=[smem] * 4 + [...  17.2 us

profile of v4, /device:TPU:56, one launch (start us, length us, event | category | flops | bytes accessed | tf_op | source)
XLA Modules:
  0.0 47.0 jit_solution(18055710378160295560)
XLA Ops:
  1.3 28.6 %exchange.1 = (f32[32,8,128]{2,1,0:T(8,128)}, f32[32,8,128]{2,1,0:T(8,128)}, f32[32,8,128]{2,1,0:T(8,128)}, s32[2,4]{1,0:T(2,128)}, s32[2,4]{1,0:T(2,128)}) custom-call(f32[96,128]{1,0:T(8,128)} %bitcast.8, f32[96,128]{1,0:T(8,128)} %bitcast.9, f32[96,128]{1,0:T(8,128)} %bitcast.10, f32[96,128]{1,0:T(8,128)} %bitcast.11, s32[32,128]{1,0:T(8,128)} %bitcast.12, ...), custom_call_target="tpu_custom_call" | custom-call | tf_op jit(solution)/shard_map/exchange/pallas_call | solution.py:204
  29.9 17.2 %pair_forces.1 = (f32[96,128]{1,0:T(8,128)}, f32[96,128]{1,0:T(8,128)}, f32[96,128]{1,0:T(8,128)}) custom-call(s32[2,1024]{1,0:T(2,128)} %pairs_ref.1, s32[1]{0:T(128)S(6)} %copy.18.count_ref, s32[2,4]{1,0:T(2,128)} %get-tuple-element.11.hlo_ref, s32[2,4]{1,0:T(2,128)} %get-tuple-element.12.hup_ref, f32[32,8,128]{2,1,0:T(8,128)} %get-tuple-element.13.pm_hbm, ...), custom_call_target="tpu_custom_call" | custom-call | tf_op jit(solution)/shard_map/pair_forces/pallas_call | solution.py:345

commit v5 on v4

--- a/solution.py
+++ b/solution.py
@@ -56,9 +56,35 @@
     return out
 
 
+def parts(rows):
+    high = rows.astype(jnp.bfloat16).astype(jnp.float32)
+    rest = rows - high
+    mid = rest.astype(jnp.bfloat16).astype(jnp.float32)
+    return high, mid, rest - mid
+
+
+def pickers():
+    row = lax.broadcasted_iota(jnp.int32, (32, LANES), 0)
+    lane = lax.broadcasted_iota(jnp.int32, (32, LANES), 1)
+    picks = [(lane == 64 * h + row) | (lane == 64 * h + 32 + row) for h in range(2)]
+    k = lax.broadcasted_iota(jnp.int32, (2 * LANES, LANES), 0)
+    n = lax.broadcasted_iota(jnp.int32, (2 * LANES, LANES), 1)
+    return picks, ((k % 64 < 32) == (n < 64)).astype(jnp.bfloat16)
+
+
+def spread(rows, hs, picks, halves):
+    lhs = [
+        jnp.concatenate([jnp.where(picks[h], p[c:c + 1], 0.0) for h in hs for c in range(rows.shape[0])],
+                        axis=0).astype(jnp.bfloat16)
+        for p in parts(rows)
+    ]
+    out = jnp.dot(jnp.concatenate(lhs[0:2], axis=1), halves, preferred_element_type=jnp.float32)
+    return out + jnp.dot(lhs[2], halves[0:LANES], preferred_element_type=jnp.float32)
+
+
 def exchange_kernel(pos_hbm, mom_hbm, frc_hbm, noise_hbm, sp_hbm, halo_hbm, fixed_hbm,
-                    pm_hbm, lo_hbm, up_hbm, hlo_hbm, hup_hbm,
-                    raw, sp_ref, fixed, out_buf, in_buf, back_buf, range_buf, load, store, send1, recv1, send2, recv2, nsend, nrecv):
+                    pm_hbm, lo_hbm, up_hbm, hlo_hbm, hup_hbm, tab_hbm,
+                    raw, tab, sp_ref, fixed, out_buf, in_buf, back_buf, range_buf, load, store, send1, recv1, send2, recv2, nsend, nrecv):
     beads = lax.axis_size("bead")
     me = lax.axis_index("bead")
     shard = lax.axis_index("space")
@@ -156,6 +182,21 @@
     each(lambda d: first(d).start())
     beside(lambda up: (lists(up).start(), bounds(up).start()))
     in_buf[pl.ds(9 * me, 9), :] = out_buf[pl.ds(9 * me, 9), :]
+    picks, halves = pickers()
+
+    def fill(t, _):
+        pair = range_buf[t]
+        sign = jnp.where(lax.broadcasted_iota(jnp.int32, pair.shape, 0) == 0, -1.0, 1.0)
+        out = spread(pair * sign, (0, 1), picks, halves)
+        for h in range(2):
+            for c in range(2):
+                s = 64 * h + 32 * c
+                tab[2 * t + h, c] = out[s:s + 32]
+        return 0
+
+    lax.fori_loop(0, range_buf.shape[0], fill, 0, unroll=4)
+    tables = pltpu.make_async_copy(tab, tab_hbm, store.at[2])
+    tables.start()
     all_rows(in_buf, 9, recv1)
 
     x = jnp.concatenate([in_buf[pl.ds(r, beads, stride=9), :] for r in range(6)], axis=1)
@@ -187,6 +228,7 @@
     beside(lambda up: all_beyond(back_buf, nsend.at[2 + int(up)]))
     beside(lambda up: all_beyond(lo_hbm if up else up_hbm, nrecv.at[2 + int(up)]), True)
     keep.wait()
+    tables.wait()
 
 
 def exchange(pos, mom, frc, noise, species, halo):
@@ -196,6 +238,7 @@
     f32 = jnp.float32
     block = jax.ShapeDtypeStruct((chunks, 8, LANES), f32)
     ids = jax.ShapeDtypeStruct(halo.shape, jnp.int32)
+    table = (2 * chunks, 2, 32, LANES)
     dma = pltpu.SemaphoreType.DMA
     fixed = np.zeros((3, beads, LANES), np.float32)
     fixed[0, :, 0:beads] = modes_matrix(beads)
@@ -203,32 +246,36 @@
     fixed[2] = mode_factors(beads)
     return pl.pallas_call(
         exchange_kernel,
-        out_shape=(block, block, block, ids, ids),
+        out_shape=(block, block, block, ids, ids, jax.ShapeDtypeStruct(table, f32)),
         in_specs=[hbm] * 7,
-        out_specs=(hbm,) * 5,
+        out_specs=(hbm,) * 6,
         scratch_shapes=[
             pltpu.VMEM((4, 3 * chunks, LANES), f32),
+            pltpu.VMEM(table, f32),
             pltpu.VMEM((chunks, LANES), jnp.int32),
             pltpu.VMEM((3 * beads, LANES), f32),
             pltpu.VMEM((beads * 9, LANES), f32),
             pltpu.VMEM((beads * 9, LANES), f32),
             pltpu.VMEM((beads, 8, LANES), f32),
             pltpu.VMEM((chunks, 2, LANES), f32),
-            dma((6,)), dma((2,)), dma, dma, dma, dma, dma((6,)), dma((6,)),
+            dma((6,)), dma((3,)), dma, dma, dma, dma, dma((6,)), dma((6,)),
         ],
-        compiler_params=pltpu.CompilerParams(collective_id=0, has_side_effects=True),
+        compiler_params=pltpu.CompilerParams(
+            collective_id=0, has_side_effects=True, vmem_limit_bytes=60 * 2**20),
         name="exchange",
     )(pos, mom, frc, noise, species, halo, jnp.asarray(fixed.reshape(3 * beads, LANES)))
 
 
-def force_kernel(pairs_ref, count_ref, hlo_ref, hup_ref, pm_hbm, lo_hbm, up_hbm, pos_ref, mom_ref, frc_ref,
-                 tab_j, tab_i, acc, pm_ref, halo, sem):
+def force_kernel(pairs_ref, count_ref, hlo_ref, hup_ref, pm_hbm, lo_hbm, up_hbm, tab_hbm, pos_ref, mom_ref, frc_ref,
+                 tab_j, tab_r, tab_i, acc, pm_ref, halo, sem):
     chunks = pm_ref.shape[0]
     blocks = 2 * chunks
     left = lax.broadcasted_iota(jnp.int32, (32, LANES), 1) < 64
     left1 = left[0:8]
     get_own = pltpu.make_async_copy(pm_hbm, pm_ref, sem.at[0])
     get_own.start()
+    get_range = pltpu.make_async_copy(tab_hbm, tab_r.at[HALO:HALO + blocks], sem.at[1 + 2 * HALO])
+    get_range.start()
     sides = []
     shard = lax.axis_index("space")
     for side in range(2):
@@ -244,37 +291,20 @@
         return 0
     lax.fori_loop(0, blocks, clear, 0, unroll=8)
     tab_j[2 * HALO + blocks] = jnp.zeros(tab_j.shape[1:], jnp.float32)
-
-    row = lax.broadcasted_iota(jnp.int32, (32, LANES), 0)
-    lane = lax.broadcasted_iota(jnp.int32, (32, LANES), 1)
-    picks = [(lane == 64 * h + row) | (lane == 64 * h + 32 + row) for h in range(2)]
-    k = lax.broadcasted_iota(jnp.int32, (2 * LANES, LANES), 0)
-    n = lax.broadcasted_iota(jnp.int32, (2 * LANES, LANES), 1)
-    halves = ((k % 64 < 32) == (n < 64)).astype(jnp.bfloat16)
+    tab_r[2 * HALO + blocks] = jnp.zeros(tab_r.shape[1:], jnp.float32)
+
+    picks, halves = pickers()
     kind = lax.broadcasted_iota(jnp.int32, (8, LANES), 0)
     factor = jnp.where(kind < 3, 1.0, jnp.where(kind < 6, ROOT, jnp.where(kind == 6, -1.0, 1.0)))
 
-    def parts(m8):
-        high = m8.astype(jnp.bfloat16).astype(jnp.float32)
-        rest = m8 - high
-        mid = rest.astype(jnp.bfloat16).astype(jnp.float32)
-        return high, mid, rest - mid
-
-    def spread_mxu(m8, hs):
-        ps = parts(m8)
-        lhs = [jnp.concatenate([jnp.where(picks[h], p[3 + c:4 + c], 0.0) for h in hs for c in range(5)], axis=0).astype(jnp.bfloat16) for p in ps]
-        both = jnp.concatenate([lhs[0], lhs[1]], axis=1)
-        out = jnp.dot(both, halves, preferred_element_type=jnp.float32)
-        return out + jnp.dot(lhs[2], halves[0:LANES], preferred_element_type=jnp.float32)
-
     get_own.wait()
 
     def own(t, _):
         m8 = pm_ref[t] * factor
-        out = spread_mxu(m8, (0, 1))
+        out = spread(m8[3:6], (0, 1), picks, halves)
         for h in range(2):
-            for c in range(5):
-                s = 160 * h + 32 * c
+            for c in range(3):
+                s = 96 * h + 32 * c
                 tab_j[HALO + 2 * t + h, c] = out[s:s + 32]
         turned = pltpu.roll(m8, 64, 1)
         for h in range(2):
@@ -290,9 +320,10 @@
         e = n_ if n_ < HALO else blocks + n_
         m8 = jnp.where(there, halo[n_], 0.0) * factor
         m8 = jnp.where(half == 1, pltpu.roll(m8, 64, 1), m8)
-        out = spread_mxu(m8, (0,))
+        out = spread(m8[3:8], (0,), picks, halves)
         for c in range(5):
-            tab_j[e, c] = out[32 * c:32 * c + 32]
+            (tab_j if c < 3 else tab_r)[e, c % 3] = out[32 * c:32 * c + 32]
+    get_range.wait()
 
     live = count_ref[0]
 
@@ -307,8 +338,8 @@
             dy = yi - tab_j[j, 1, s]
             dz = zi - tab_j[j, 2, s]
             d = dx * dx + dy * dy + dz * dz
-            inv = 1.0 / (ri + tab_j[j, 3, s])
-            w = jnp.exp2(d * inv) * (inv * tab_j[j, 4, s])
+            inv = 1.0 / (ri + tab_r[j, 0, s])
+            w = jnp.exp2(d * inv) * (inv * tab_r[j, 1, s])
             for k, v in enumerate((dx, dy, dz)):
                 f[k] = w * v if g == 0 else f[k] + w * v
         return i, f
@@ -336,7 +367,7 @@
     lax.fori_loop(0, chunks, finish, 0, unroll=8)
 
 
-def force_call(pairs, count, hlo, hup, pm, lo, up):
+def force_call(pairs, count, hlo, hup, pm, lo, up, tab):
     chunks = pm.shape[0]
     smem = pl.BlockSpec(memory_space=pltpu.SMEM)
     vmem = pl.BlockSpec(memory_space=pltpu.VMEM)
@@ -345,25 +376,26 @@
     return pl.pallas_call(
         force_kernel,
         out_shape=(o, o, o),
-        in_specs=[smem] * 4 + [hbm] * 3,
+        in_specs=[smem] * 4 + [hbm] * 4,
         out_specs=(vmem,) * 3,
         scratch_shapes=[
-            pltpu.VMEM((2 * chunks + 2 * HALO + 1, 5, 32, LANES), jnp.float32),
+            pltpu.VMEM((2 * chunks + 2 * HALO + 1, 3, 32, LANES), jnp.float32),
+            pltpu.VMEM((2 * chunks + 2 * HALO + 1, 2, 32, LANES), jnp.float32),
             pltpu.VMEM((2 * chunks, 4, 8, LANES), jnp.float32),
             pltpu.VMEM((2 * chunks, 24, LANES), jnp.float32),
             pltpu.VMEM((chunks, 8, LANES), jnp.float32),
             pltpu.VMEM((2 * HALO, 8, LANES), jnp.float32),
-            pltpu.SemaphoreType.DMA((1 + 2 * HALO,)),
+            pltpu.SemaphoreType.DMA((2 + 2 * HALO,)),
         ],
         compiler_params=pltpu.CompilerParams(vmem_limit_bytes=60 * 2**20),
         name="pair_forces",
-    )(pairs, count, hlo, hup, pm, lo, up)
+    )(pairs, count, hlo, hup, pm, lo, up, tab)
 
 
 def shards(positions, momenta, forces, noise, species, block_pairs, pair_count, halo_blocks):
     flat = [a.reshape(-1, LANES) for a in (positions, momenta, forces, noise)]
-    pm, lo, up, hlo, hup = exchange(*flat, species.reshape(-1, LANES), halo_blocks)
-    outs = force_call(block_pairs, pair_count, hlo, hup, pm, lo, up)
+    pm, lo, up, hlo, hup, tab = exchange(*flat, species.reshape(-1, LANES), halo_blocks)
+    outs = force_call(block_pairs, pair_count, hlo, hup, pm, lo, up, tab)
     return tuple(o.reshape(positions.shape) for o in outs)
 
 

time: 47.3 us -> 48.4 us (1.023)
  the two profiles are of different devices: /device:TPU:56 before, /device:TPU:33 now
where the time goes in v5:
time: 48.4 us; the launch traced here: 48.1 us
  Pallas kernels  46.8 us (97%)
  between operations  1.29 us (3%)
    pallas_call x1, Pallas kernels, exchange(): pl.pallas_call(exchange_kernel, out_shape=(block, block, block, ids, ids,...  30.5 us
    pallas_call x1, Pallas kernels, force_call(): pl.pallas_call(force_kernel, out_shape=(o, o, o), in_specs=[smem] * 4 + [...  16.3 us

profile of v5, /device:TPU:33, one launch (start us, length us, event | category | flops | bytes accessed | tf_op | source)
XLA Modules:
  0.0 48.1 jit_solution(12941175035203275819)
XLA Ops:
  1.3 30.5 %exchange.1 = (f32[32,8,128]{2,1,0:T(8,128)}, f32[32,8,128]{2,1,0:T(8,128)}, f32[32,8,128]{2,1,0:T(8,128)}, s32[2,4]{1,0:T(2,128)}, s32[2,4]{1,0:T(2,128)}, /*index=5*/f32[64,2,32,128]{3,2,1,0:T(8,128)}) custom-call(f32[96,128]{1,0:T(8,128)} %bitcast.8, f32[96,128]{1,0:T(8,128)} %bitcast.9, f32[96,128]{1,0:T(8,128)} %bitcast.10, f32[96,128]{1,0:T(8,128)} %bitcast.11, ...), custom_call_target="tpu_custom_call" | custom-call | tf_op jit(solution)/shard_map/exchange/pallas_call | solution.py:247
  31.8 16.3 %pair_forces.1 = (f32[96,128]{1,0:T(8,128)}, f32[96,128]{1,0:T(8,128)}, f32[96,128]{1,0:T(8,128)}) custom-call(s32[2,1024]{1,0:T(2,128)} %pairs_ref.1, s32[1]{0:T(128)S(6)} %copy.18.count_ref, s32[2,4]{1,0:T(2,128)} %get-tuple-element.12.hlo_ref, s32[2,4]{1,0:T(2,128)} %get-tuple-element.13.hup_ref, f32[32,8,128]{2,1,0:T(8,128)} %get-tuple-element.14.pm_hbm, ...), custom_call_target="tpu_custom_call" | custom-call | tf_op jit(solution)/shard_map/pair_forces/pallas_call | solution.py:376
